TPU v7x, 32 devices: a whole 2x2x4 slice. The times are simulated.
32 devices in a mesh: seq: 4 (over x, core), exp: 8 (over z, y).
Axes of the slice: x: 2, y: 2, z: 4, core: 2. Of those that a mesh axis runs over, the one named last changes fastest.
Arguments:
- queries: bfloat16 [8, 512, 2048], P('exp', 'seq'), may hold values from -14 to 14
- keys: bfloat16 [8, 512, 2048], P('exp', 'seq'), may hold values from -6 to 6
- values: bfloat16 [8, 512, 2048], P('exp', 'seq'), may hold values from -6 to 6
- out_grad: bfloat16 [8, 512, 2048], P('exp', 'seq'), may hold values from -6 to 6
- norm_gain: float32 [2048], replicated, may hold values from 0.5 to 1.5
- gate_values: float32 [8, 512, 2], P('exp', 'seq'), may hold values from 0.2 to 1
- expert_ids: int32 [8, 512, 2], P('exp', 'seq'), may hold values from 0 to 15, all different within a row; in each aligned block of 128 rows (0 to 127, 128 to 255, ..., all dimensions but the last counted through in order) at most 20 rows name the same one
- tile_offsets: int32 [8, 8, 3], P('exp', 'seq'), may hold values from -2 to 2, as said below
- gate_weight: bfloat16 [8, 4, 2048, 1024], P('exp', 'seq'), may hold values from -0.125 to 0.125
- up_weight: bfloat16 [8, 4, 2048, 1024], P('exp', 'seq'), may hold values from -0.125 to 0.125
- down_weight: bfloat16 [8, 4, 1024, 2048], P('exp', 'seq'), may hold values from -0.125 to 0.125
Outputs:
- key_grad: bfloat16 [8, 512, 2048], P('exp', 'seq')
- value_grad: bfloat16 [8, 512, 2048], P('exp', 'seq')
Inputs may be any that keep to these rules, and one draw needn't show every extreme that they name: `expert_ids`: a token's two ids differ; the tokens of one index pair (one device) name one expert at most 20 times. `tile_offsets`: each row holds 3 different offsets, the first of them 0.
All inputs are finite; a program needn't handle non-finite values.
Results may differ from a plain program's by a relative error of at most 0.013.
Values may be sent and summed in bfloat16 or wider, within the bound.
A program may use at most 128 MiB of HBM per device.

v0:
```python
import jax
import jax.numpy as jnp
from jax import lax
from jax.sharding import PartitionSpec as P

HEAD_DIM = 128
TILE = 64


epsilon = 1e-06


def with_halo(cells, sides, width):
    for axis, dim in sides:
        count = lax.axis_size(axis)
        ends = count - 1
        head = lax.slice_in_dim(cells, 0, width, axis=dim)
        tail = lax.slice_in_dim(cells, cells.shape[dim] - width, cells.shape[dim], axis=dim)
        cells = jnp.concatenate(
            [
                lax.ppermute(tail, axis, [(i, (i + 1) % count) for i in range(ends)]),
                cells,
                lax.ppermute(head, axis, [((i + 1) % count, i) for i in range(ends)]),
            ],
            axis=dim,
        )
    return cells


def expert_part(rows_in, rows_grad, gate_w, up_w, down_w):
    part_width = gate_w.shape[1]
    both_w = jnp.concatenate([gate_w, up_w], axis=1)
    projected = jnp.dot(rows_in, both_w, preferred_element_type=jnp.float32)
    gate_proj = projected[:, :part_width]
    up_proj = projected[:, part_width:]
    hidden_grad = jnp.einsum("rd,fd->rf", rows_grad, down_w, preferred_element_type=jnp.float32)
    sig = jax.nn.sigmoid(gate_proj)
    grad_up = (hidden_grad * gate_proj * sig).astype(jnp.bfloat16)
    grad_gate = (hidden_grad * up_proj * sig * (1.0 + gate_proj * (1.0 - sig))).astype(jnp.bfloat16)
    both_grad = jnp.concatenate([grad_gate, grad_up], axis=1)
    total = jnp.einsum("rf,df->rd", both_grad, both_w, preferred_element_type=jnp.float32)
    return total.astype(jnp.bfloat16)


def on_device(
    queries,
    keys,
    values,
    out_grad,
    norm_gain,
    gate_values,
    expert_ids,
    tile_offsets,
    gate_weight,
    up_weight,
    down_weight,
):
    query_rows = queries[0]
    local_len, width = query_rows.shape
    heads = width // HEAD_DIM
    local_tiles = local_len // TILE
    halo_tiles = 2
    halo_len = halo_tiles * TILE
    ext_tiles = local_tiles + 2 * halo_tiles
    seq_count = lax.axis_size("seq")
    col_count = lax.axis_size("exp")
    group = seq_count // 2
    expert_count = 2 * col_count
    capacity = max(2, (5 * local_len + 2 * expert_count - 1) // (2 * expert_count))
    scale = HEAD_DIM ** (-0.5)
    key_value = jnp.stack([keys[0], values[0]])
    extended = with_halo(key_value, (("seq", 1),), halo_len)
    offsets = tile_offsets[0]
    neighbour_count = offsets.shape[1]
    tile_base = jnp.arange(local_tiles, dtype=jnp.int32)[:, None]
    ext_index = tile_base + halo_tiles + offsets
    global_tile = lax.axis_index("seq") * local_tiles + tile_base + offsets
    valid = (global_tile >= 0) & (global_tile < local_tiles * seq_count)
    key_mask = jnp.repeat(valid, TILE, axis=1)
    tile_shape = (ext_tiles, TILE, heads, HEAD_DIM)
    window_shape = (local_tiles, neighbour_count * TILE, heads, HEAD_DIM)
    key_tiles = extended[0].reshape(tile_shape)[ext_index].reshape(window_shape)
    value_tiles = extended[1].reshape(tile_shape)[ext_index].reshape(window_shape)
    query_tiles = query_rows.reshape(local_tiles, TILE, heads, HEAD_DIM)
    scores = (
        jnp.einsum("tqhd,tkhd->thqk", query_tiles, key_tiles, preferred_element_type=jnp.float32)
        * scale
    )
    scores = jnp.where(key_mask[:, None, None, :], scores, -jnp.inf)
    row_max = jnp.max(scores, axis=-1, keepdims=True)
    raised = jnp.exp(scores - row_max)
    attn_weights = raised / jnp.sum(raised, axis=-1, keepdims=True)
    weights_b = attn_weights.astype(jnp.bfloat16)
    attn_out = jnp.einsum(
        "thqk,tkhd->tqhd", weights_b, value_tiles, preferred_element_type=jnp.float32
    )
    attn_out = attn_out.reshape(local_len, width)
    inv_rms = lax.rsqrt(jnp.mean(attn_out * attn_out, axis=-1, keepdims=True) + epsilon)
    unit = attn_out * inv_rms
    normed = (unit * norm_gain).astype(jnp.bfloat16)
    grad_rows = out_grad[0]
    route_experts = expert_ids[0].reshape(-1)
    one_hot = (route_experts[:, None] == jnp.arange(expert_count, dtype=jnp.int32)[None, :]).astype(
        jnp.int32
    )
    rank_index = jnp.sum(jnp.cumsum(one_hot, axis=0) * one_hot, axis=1) - 1
    route_token = jnp.arange(2 * local_len, dtype=jnp.int32) // 2
    token_pair = jnp.stack([normed, grad_rows])
    route_pair = token_pair[:, route_token]
    part_gate = gate_weight[0, 0]
    part_up = up_weight[0, 0]
    part_down = down_weight[0, 0]
    half_index = route_experts % 2
    column = route_experts // 2
    slot_index = half_index * (col_count * capacity) + column * capacity + rank_index
    empty = jnp.zeros((2, 2 * col_count * capacity, width), jnp.bfloat16)
    send_pair = empty.at[:, slot_index].set(route_pair).reshape(2, 2, col_count, capacity, width)
    spread_pair = jnp.repeat(send_pair, group, axis=1)
    half_pair = lax.all_to_all(spread_pair, "seq", split_axis=1, concat_axis=1, tiled=True)
    expert_pair = lax.all_to_all(half_pair, "exp", split_axis=2, concat_axis=2, tiled=True)
    partial_value = expert_part(
        expert_pair[0].reshape(-1, width),
        expert_pair[1].reshape(-1, width),
        part_gate,
        part_up,
        part_down,
    )
    partial_value = partial_value.reshape(seq_count, col_count, capacity, width)
    backed = lax.all_to_all(partial_value, "exp", split_axis=1, concat_axis=1, tiled=True)
    homed = lax.all_to_all(backed, "seq", split_axis=0, concat_axis=0, tiled=True)
    summed = jnp.sum(homed.reshape(2, group, col_count, capacity, width), axis=1, dtype=jnp.float32)
    route_grad = summed.astype(jnp.bfloat16).reshape(2 * col_count * capacity, width)[slot_index]
    route_grad = route_grad.reshape(local_len, 2, width).astype(jnp.float32)
    normed_grad = jnp.sum(gate_values[0][:, :, None] * route_grad, axis=1)
    scaled = normed_grad * norm_gain
    attn_grad = grad_rows.astype(jnp.float32) + inv_rms * (
        scaled - unit * jnp.mean(scaled * unit, axis=-1, keepdims=True)
    )
    attn_grad_b = attn_grad.astype(jnp.bfloat16).reshape(local_tiles, TILE, heads, HEAD_DIM)
    prob_grad = jnp.einsum(
        "tqhd,tkhd->thqk", attn_grad_b, value_tiles, preferred_element_type=jnp.float32
    )
    inner_sum = jnp.sum(attn_weights * prob_grad, axis=-1, keepdims=True)
    score_grad = (attn_weights * (prob_grad - inner_sum)).astype(jnp.bfloat16)
    key_part = (
        jnp.einsum("thqk,tqhd->tkhd", score_grad, query_tiles, preferred_element_type=jnp.float32)
        * scale
    )
    value_part = jnp.einsum(
        "thqk,tqhd->tkhd", weights_b, attn_grad_b, preferred_element_type=jnp.float32
    )
    flat_index = ext_index.reshape(-1)
    part_shape = (local_tiles * neighbour_count, TILE, heads, HEAD_DIM)
    ext_grad = jnp.zeros((2, ext_tiles, TILE, heads, HEAD_DIM), jnp.float32)
    ext_grad = ext_grad.at[0, flat_index].add(key_part.reshape(part_shape))
    ext_grad = ext_grad.at[1, flat_index].add(value_part.reshape(part_shape))
    ext_grad = ext_grad.reshape(2, ext_tiles * TILE, width)
    rims = jnp.concatenate([ext_grad[:, :halo_len], ext_grad[:, -halo_len:]], axis=1)
    rims_in = with_halo(rims, (("seq", 1),), halo_len)
    inner_grad = ext_grad[:, halo_len : halo_len + local_len]
    inner_grad = inner_grad.at[:, :halo_len].add(rims_in[:, :halo_len])
    inner_grad = inner_grad.at[:, local_len - halo_len :].add(rims_in[:, -halo_len:])
    key_out = inner_grad[0].astype(jnp.bfloat16)[None]
    value_out = inner_grad[1].astype(jnp.bfloat16)[None]
    return (key_out, value_out)


def solution(mesh):
    return jax.shard_map(
        on_device,
        mesh=mesh,
        in_specs=(
            P("exp", "seq", None),
            P("exp", "seq", None),
            P("exp", "seq", None),
            P("exp", "seq", None),
            P(),
            P("exp", "seq", None),
            P("exp", "seq", None),
            P("exp", "seq", None),
            P("exp", "seq", None, None),
            P("exp", "seq", None, None),
            P("exp", "seq", None, None),
        ),
        out_specs=(P("exp", "seq", None), P("exp", "seq", None)),
        check_vma=False,
    )
```

profile of v0, /device:TPU:1, one launch (start us, length us, event | category | flops | bytes accessed | tf_op | source)
XLA Modules:
  0.0 492.9 jit_solution(1804225258380720316)
XLA Ops:
  4.8 4.5 collective-permute-start
  15.1 4.6 collective-permute-done.1
  34.4 10.5 %gather_fusion.2 = bf16[256,2,2048]{2,1,0:T(2,128)(2,1)} fusion(bf16[2,128,2048]{2,0,1:T(2,128)(2,1)S(1)} %copy.92, s32[1024]{0:T(1024)S(1)} %get-tuple-element.61), kind=kCustom, calls=%fused_computation.2 | custom fusion | bytes 4195328 | tf_op jit(solution)/shard_map/gather | solution.py:109
  46.3 21.6 %scatter_fusion = bf16[2,320,2048]{2,0,1:T(2,128)(2,1)S(1)} fusion(bf16[2,320,2048]{2,0,1:T(2,128)(2,1)S(1)} %broadcast_in_dim.27, s32[256]{0:T(256)S(1)} %bitcast.116, bf16[256,2,2048]{2,1,0:T(2,128)(2,1)} %gather_fusion.2), kind=kCustom, calls=%fused_computation.4 | custom fusion | bytes 6292480 | tf_op jit(solution)/shard_map/scatter | solution.py:117
  70.1 62.3 %all_to_all.20 = bf16[2,4,8,20,2048]{4,2,3,0,1:T(8,128)(2,1)S(1)} all-to-all(bf16[2,4,8,20,2048]{4,2,3,0,1:T(8,128)(2,1)S(1)} %bitcast.97), channel_id=1, replica_groups=mesh['seq'=4,'exp'=8] {'seq'}, dimensions={1} | all-to-all | bytes 10485760 | tf_op jit(solution)/shard_map/all_to_all | solution.py:119
  132.4 4.0 copy.94
  136.4 120.4 %all_to_all.21 = bf16[2,4,8,20,2048]{4,1,3,0,2:T(4,128)(2,1)S(1)} all-to-all(bf16[2,4,8,20,2048]{4,1,3,0,2:T(4,128)(2,1)S(1)} %copy.94), channel_id=1, replica_groups=mesh['seq'=4,'exp'=8] {'exp'}, dimensions={2} | all-to-all | bytes 10485760 | tf_op jit(solution)/shard_map/all_to_all | solution.py:120
  256.8 5.4 %fusion.47 = (bf16[1,4,8,20,2048]{4,1,3,0,2:T(4,128)(2,1)S(1)}, bf16[1,4,8,20,2048]{4,1,3,0,2:T(4,128)(2,1)}) fusion(bf16[2,4,8,20,2048]{4,1,3,0,2:T(4,128)(2,1)S(1)} %all_to_all.21), kind=kLoop, calls=%fused_computation.110 | loop fusion | bytes 10485760 | tf_op jit(solution)/shard_map/slice | solution.py:122
  265.8 3.2 copy.95
  271.3 9.1 %fusion.2 = f32[640,2048]{1,0:T(8,128)S(1)} fusion(bf16[640,2048]{1,0:T(8,128)(2,1)} %reshape_squeeze.23, bf16[2048,1024]{1,0:T(8,128)(2,1)} %bitcast.120, bf16[2048,1024]{1,0:T(8,128)(2,1)} %bitcast.122), kind=kOutput, calls=%fused_computation.10 | convolution fusion | flops 5385486336 | bytes 16252928 | tf_op jit(solution)/shard_map/dot_general | solution.py:33
  280.4 3.6 fusion.8
  284.1 18.6 %fusion.5 = bf16[640,2048]{1,0:T(8,128)(2,1)} fusion(bf16[2048,1024]{1,0:T(8,128)(2,1)S(1)} %bitcast.121, bf16[2048,1024]{1,0:T(8,128)(2,1)S(1)} %bitcast.123, bf16[640,1024]{1,0:T(8,128)(2,1)S(1)} %get-tuple-element.45, bf16[640,1024]{1,0:T(8,128)(2,1)S(1)} %get-tuple-element.44), kind=kOutput, calls=%fused_computation.13 | convolution fusion | flops 5392039936 | bytes 13631488 | tf_op jit(solution)/shard_map/rf,df->rd/dot_general | solution.py:41
  302.7 3.5 reshape.494
  308.2 62.1 %all_to_all.22 = bf16[4,8,20,2048]{3,0,2,1:T(4,128)(2,1)S(1)} all-to-all(bf16[4,8,20,2048]{3,0,2,1:T(4,128)(2,1)S(1)} %copy.97), channel_id=1, replica_groups=mesh['seq'=4,'exp'=8] {'exp'}, dimensions={1} | all-to-all | bytes 5242880 | tf_op jit(solution)/shard_map/all_to_all | solution.py:129
  373.3 5.7 %all-to-all-start.3 = ((bf16[4,8,20,2048]{3,1,2,0:T(8,128)(2,1)}), bf16[4,8,20,2048]{3,1,2,0:T(8,128)(2,1)S(1)}, u32[]{:S(2)}, u32[]{:S(2)}) async-start(bf16[4,8,20,2048]{3,1,2,0:T(8,128)(2,1)} %copy.98), calls=%async_computation.3 | async-start | bytes 5242880 | tf_op jit(solution)/shard_map/all_to_all | solution.py:130
  380.7 28.8 %all-to-all-done.3 = bf16[4,8,20,2048]{3,1,2,0:T(8,128)(2,1)S(1)} async-done(((bf16[4,8,20,2048]{3,1,2,0:T(8,128)(2,1)}), bf16[4,8,20,2048]{3,1,2,0:T(8,128)(2,1)S(1)}, u32[]{:S(2)}, u32[]{:S(2)}) %all-to-all-start.3) | async-done | bytes 2621472 | tf_op jit(solution)/shard_map/all_to_all | solution.py:130
  413.9 3.2 multiply_reduce_fusion.1
  424.8 3.5 copy.104
  430.2 3.3 broadcast_in_dim.22
  433.5 8.7 %scatter_fusion.1 = f32[2,6,64,16,128]{4,3,2,1,0:T(8,128)} fusion(f32[2,6,64,16,128]{4,3,2,1,0:T(8,128)} %broadcast_in_dim.22, s32[6]{0:T(128)S(1)} %select_bitcast_fusion.1, f32[6,64,16,128]{3,2,1,0:T(8,128)} %bitcast.100), kind=kCustom, calls=%fused_computation.5 | custom fusion | flops 786432 | bytes 9437232 | tf_op jit(solution)/shard_map/scatter-add | solution.py:155
  442.2 7.6 %scatter_fusion.2 = f32[2,6,64,16,128]{4,3,2,1,0:T(8,128)} fusion(f32[2,6,64,16,128]{4,3,2,1,0:T(8,128)} %scatter_fusion.1, s32[6]{0:T(128)S(1)} %get-tuple-element.42, f32[6,64,16,128]{3,2,1,0:T(8,128)S(1)} %bitcast.99), kind=kCustom, calls=%fused_computation.6 | custom fusion | flops 786432 | bytes 9437232 | tf_op jit(solution)/shard_map/scatter-add | solution.py:156
  449.8 7.1 %reshape.499 = f32[2,384,2048]{2,1,0:T(8,128)} reshape(f32[2,6,64,16,128]{4,3,2,1,0:T(8,128)} %scatter_fusion.2) | data formatting | bytes 12582912 | tf_op jit(solution)/shard_map/reshape | solution.py:157
  464.0 21.0 %collective-permute-done.2 = f32[2,128,2048]{2,1,0:T(8,128)S(1)} collective-permute-done((f32[2,128,2048]{2,1,0:T(8,128)S(1)}, f32[2,128,2048]{2,1,0:T(8,128)S(1)}, u32[]{:S(2)}, u32[]{:S(2)}) %collective-permute-start.2) | collective-permute-done | bytes 2097184 | tf_op jit(solution)/shard_map/ppermute | solution.py:21
  485.1 4.4 collective-permute-done.3
  (111 shorter events, 64.6 us)
Async XLA Ops:
  2.8 17.0 %collective-permute-start.1 = (bf16[2,128,2048]{2,1,0:T(8,128)(2,1)S(1)}, bf16[2,128,2048]{2,1,0:T(8,128)(2,1)S(1)}, u32[]{:S(2)}, u32[]{:S(2)}) collective-permute-start(bf16[2,128,2048]{2,1,0:T(8,128)(2,1)S(1)} %constant_dynamic-update-slice_fusion), channel_id=1, source_target_pairs={{8,0},{16,8},{24,16},{9,1},{17,9},{25,17},{10,2},{18,10},{26,18},{... | collective-permute-start | bytes 3145736 | tf_op jit(solution)/shard_map/ppermute | solution.py:23
  4.8 16.2 %collective-permute-start = (bf16[2,128,2048]{2,1,0:T(8,128)(2,1)S(1)}, bf16[2,128,2048]{2,1,0:T(8,128)(2,1)S(1)}, u32[]{:S(2)}, u32[]{:S(2)}) collective-permute-start(bf16[2,128,2048]{2,1,0:T(8,128)(2,1)S(1)} %constant_dynamic-update-slice_fusion), channel_id=1, source_target_pairs={{0,8},{8,16},{16,24},{1,9},{9,17},{17,25},{2,10},{10,18},{18,26},{... | collective-permute-start | bytes 3145736 | tf_op jit(solution)/shard_map/ppermute | solution.py:21
  24.4 2.0 copy-start.2
  28.6 1.4 copy-start.7
  29.6 1.5 copy-start.15
  31.1 1.1 copy-start
  31.1 0.9 copy-start.9
  271.3 9.1 %copy-start.4 = (bf16[640,2048]{1,0:T(8,128)(2,1)S(1)}, bf16[640,2048]{1,0:T(8,128)(2,1)}, u32[]{:S(2)}) copy-start(bf16[640,2048]{1,0:T(8,128)(2,1)} %reshape_squeeze.22) | copy-start | bytes 7864324
  271.3 9.1 %copy-start.12 = (bf16[1,1,1024,2048]{3,2,1,0:T(8,128)(2,1)S(1)}, bf16[1,1,1024,2048]{3,2,1,0:T(8,128)(2,1)}, u32[]{:S(2)}) copy-start(bf16[1,1,1024,2048]{3,2,1,0:T(8,128)(2,1)} %param.29) | copy-start | bytes 12582916
  280.4 3.6 copy-start.13
  280.4 3.6 copy-start.14
  373.3 5.7 %copy-start.10 = (s32[1,2,3]{2,1,0:T(2,128)S(1)}, s32[1,2,3]{2,1,0:T(2,128)}, u32[]{:S(2)}) copy-start(s32[1,2,3]{2,1,0:T(2,128)} %param.26) | copy-start | bytes 76
  373.3 6.0 %copy-start.11 = (f32[1,128,2]{1,2,0:T(2,128)S(1)}, f32[1,128,2]{1,2,0:T(2,128)}, u32[]{:S(2)}) copy-start(f32[1,128,2]{1,2,0:T(2,128)} %param.24) | copy-start | bytes 3076
  373.3 6.1 %copy-start.5 = (bf16[1,128,2048]{2,1,0:T(8,128)(2,1)S(1)}, bf16[1,128,2048]{2,1,0:T(8,128)(2,1)}, u32[]{:S(2)}) copy-start(bf16[1,128,2048]{2,1,0:T(8,128)(2,1)} %param.22) | copy-start | bytes 1572868
  373.3 36.2 %all-to-all-start.3 = ((bf16[4,8,20,2048]{3,1,2,0:T(8,128)(2,1)}), bf16[4,8,20,2048]{3,1,2,0:T(8,128)(2,1)S(1)}, u32[]{:S(2)}, u32[]{:S(2)}) async-start(bf16[4,8,20,2048]{3,1,2,0:T(8,128)(2,1)} %copy.98), calls=%async_computation.3 | async-start | bytes 5242880 | tf_op jit(solution)/shard_map/all_to_all | solution.py:130
  413.8 3.4 copy-start.1
  417.0 1.2 copy-start.3
  417.3 1.8 copy-start.8
  417.3 2.2 copy-start.16
  420.9 1.3 copy-start.6
  459.3 25.7 %collective-permute-start.2 = (f32[2,128,2048]{2,1,0:T(8,128)S(1)}, f32[2,128,2048]{2,1,0:T(8,128)S(1)}, u32[]{:S(2)}, u32[]{:S(2)}) collective-permute-start(f32[2,128,2048]{2,1,0:T(8,128)S(1)} %get-tuple-element.46), channel_id=1, source_target_pairs={{0,8},{8,16},{16,24},{1,9},{9,17},{17,25},{2,10},{10,18},{18,26},{... | collective-permute-start | bytes 6291464 | tf_op jit(solution)/shard_map/ppermute | solution.py:21
  462.1 27.4 %collective-permute-start.3 = (f32[2,128,2048]{2,1,0:T(8,128)S(1)}, f32[2,128,2048]{2,1,0:T(8,128)S(1)}, u32[]{:S(2)}, u32[]{:S(2)}) collective-permute-start(f32[2,128,2048]{2,1,0:T(8,128)S(1)} %get-tuple-element.47), channel_id=1, source_target_pairs={{8,0},{16,8},{24,16},{9,1},{17,9},{25,17},{10,2},{18,10},{26,18},{... | collective-permute-start | bytes 6291464 | tf_op jit(solution)/shard_map/ppermute | solution.py:23
where the time goes:
time: 503 us; the launch traced here: 493 us
  blocking collectives  245 us (49%)
  local copies, waits for them, and re-layouts  102 us (20%)
  waiting for transfers between devices  60 us (12%)
  matrix products  39.8 us (8%)
  other arithmetic  28.3 us (6%)
  starting transfers between devices  16.8 us (3%)
    all_to_all x1, blocking collectives, on_device(): lax.all_to_all(half_pair, 'exp', split_axis=2, concat_axis=2, tiled=True)  120 us
    all_to_all x1, blocking collectives, on_device(): lax.all_to_all(spread_pair, 'seq', split_axis=1, concat_axis=1, tiled=True)  62.3 us
    all_to_all x1, blocking collectives, on_device(): lax.all_to_all(partial_value, 'exp', split_axis=1, concat_axis=1, tiled=T...  62.1 us
    all_to_all x1, waiting for transfers between devices, on_device(): lax.all_to_all(backed, 'seq', split_axis=0, concat_axis=0, tiled=True)  28.8 us
    ppermute x2, waiting for transfers between devices, with_halo(): lax.ppermute(tail, axis, [(i, (i + 1) % count) for i in range(ends)])  22.2 us
    scatter x1, local copies, waits for them, and re-layouts, on_device(): empty.at[:, slot_index].set(route_pair)  21.6 us
    dot_general x1, matrix products, expert_part(): jnp.einsum('rf,df->rd', both_grad, both_w, preferred_element_type=jnp.flo...  18.6 us
    gather x1, local copies, waits for them, and re-layouts, on_device(): route_pair = token_pair[:, route_token]  10.5 us
  transfers between devices with their start and end apart: 5, of which 5 were waited for; matrix products, arithmetic and copies ran while one was open for 2% of the time, Pallas kernels for 0%

commit v1 on v0

v1 whole, which is shorter than its diff:
```python
import functools

import jax
import jax.numpy as jnp
from jax import lax
from jax.experimental import pallas as pl
from jax.experimental.pallas import tpu as pltpu
from jax.sharding import PartitionSpec as P

HEAD_DIM = 128
TILE = 64
SUB = 16
MESH = pl.DeviceIdType.MESH

epsilon = 1e-06


def dot(a, b, dims=((1,), (0,))):
    return lax.dot_general(a, b, (dims, ((), ())), preferred_element_type=jnp.float32)


def iota(shape, dim):
    return lax.broadcasted_iota(jnp.int32, shape, dim)


class Plan:
    def __init__(self, local_len, width, seq_count, col_count):
        self.local_len, self.width = local_len, width
        self.seq_count, self.col_count = seq_count, col_count
        self.group = seq_count // 2
        self.heads = width // HEAD_DIM
        experts = 2 * col_count
        capacity = max(2, (5 * local_len + 2 * experts - 1) // (2 * experts))
        self.full = capacity // SUB
        left = capacity % SUB
        self.rest = 0 if left == 0 else 4 if left <= 4 else 8 if left <= 8 else 16
        if self.rest == 16:
            self.full, self.rest = self.full + 1, 0
        self.cuts = SUB // self.rest if self.rest else 0
        self.cut = width // self.cuts if self.rest else 0
        self.packed = self.full * width + self.cut
        self.dests = 2 * col_count
        self.rows = self.dests * SUB
        self.pieces = 4


def expert_of(plan, dest):
    return 2 * (dest % plan.col_count) + dest // plan.col_count


def partner(plan, dest, member):
    return (dest // plan.col_count * plan.group + member, dest % plan.col_count)


def place():
    return lax.axis_index("seq"), lax.axis_index("exp")


def crosses(plan, seq, side):
    other = seq + side
    return (other >= 0) & (other < plan.seq_count) & (other // plan.group != seq // plan.group)


def greet(plan):
    seq, exp = place()
    member = seq % plan.group
    mine = seq // plan.group * plan.col_count + exp
    barrier = pltpu.get_barrier_semaphore()

    def step(j, carry):
        dest = (mine + j) % plan.dests
        pl.semaphore_signal(barrier, inc=1, device_id=partner(plan, dest, member), device_id_type=MESH)
        return carry

    lax.fori_loop(1, plan.dests, step, 0)
    for other in range(1, plan.group):
        to = seq // plan.group * plan.group + (member + other) % plan.group
        pl.semaphore_signal(barrier, inc=1, device_id=(to, exp), device_id_type=MESH)
    low, high = crosses(plan, seq, -1), crosses(plan, seq, 1)

    @pl.when(low)
    def _():
        pl.semaphore_signal(barrier, inc=1, device_id=(seq - 1, exp), device_id_type=MESH)

    @pl.when(high)
    def _():
        pl.semaphore_signal(barrier, inc=1, device_id=(seq + 1, exp), device_id_type=MESH)

    peers = plan.dests - 1 + plan.group - 1
    pl.semaphore_wait(barrier, peers + jnp.where(low, 1, 0) + jnp.where(high, 1, 0))


def remote(src, dst, send, recv, to):
    return pltpu.make_async_remote_copy(
        src_ref=src, dst_ref=dst, send_sem=send, recv_sem=recv, device_id=to, device_id_type=MESH
    )


def window_mask(plan, offs_ref, seq):
    tiles = plan.local_len // TILE
    key_tile = iota((3 * plan.local_len, plan.local_len), 0) // TILE
    query_tile = iota((3 * plan.local_len, plan.local_len), 1) // TILE
    mask = jnp.zeros((3 * plan.local_len, plan.local_len), jnp.int32)
    for i in range(tiles):
        for m in range(offs_ref.shape[1]):
            offset = offs_ref[i, m]
            whole = seq * tiles + i + offset
            inside = (whole >= 0) & (whole < tiles * plan.seq_count)
            target = jnp.where(inside, tiles + i + offset, -1)
            mask = mask | ((query_tile == i) & (key_tile == target)).astype(jnp.int32)
    return mask > 0


def forward_kernel(
    plan, offs_ref, ids_ref, q_ref, k_ref, v_ref, grad_ref, gain_ref,
    recv_ref, prob_ref, unit_ref, inv_ref, vx_ref,
    kx_ref, normed_ref, sbuf, out_ref,
    halo_send, halo_recv, send_sem, recv_sem, fsend, frecv,
):
    seq, exp = place()
    local_len, width, rows = plan.local_len, plan.width, plan.rows
    member = seq % plan.group
    mine = seq // plan.group * plan.col_count + exp
    last = plan.seq_count - 1
    greet(plan)

    def halo(right):
        to = (seq + 1, exp) if right else (seq - 1, exp)
        slot = 0 if right else 2
        d = 0 if right else 1
        return [
            remote(ref, ext.at[slot], halo_send.at[i, d], halo_recv.at[i, d], to)
            for i, (ref, ext) in enumerate(((k_ref, kx_ref), (v_ref, vx_ref)))
        ]

    @pl.when(seq < last)
    def _():
        for c in halo(True):
            c.start()

    @pl.when(seq > 0)
    def _():
        for c in halo(False):
            c.start()

    expert = expert_of(plan, iota((plan.dests, local_len), 0))
    routed = ((ids_ref[0:1, :] == expert) | (ids_ref[1:2, :] == expert)).astype(jnp.float32)
    before = (iota((local_len, local_len), 0) < iota((local_len, local_len), 1)).astype(jnp.bfloat16)
    rank = dot(routed.astype(jnp.bfloat16), before)
    held = jnp.where(routed > 0, rank, -1.0).astype(jnp.bfloat16)
    spread = (iota((rows, plan.dests), 0) // SUB == iota((rows, plan.dests), 1)).astype(jnp.bfloat16)
    slot_of = dot(spread, held).astype(jnp.int32)
    row = iota((rows, local_len), 0) % SUB

    def pack(which, rows_ref):
        for f in range(plan.full):
            pick = (slot_of == row + f * SUB).astype(jnp.bfloat16)
            sbuf[which, :, f * width : (f + 1) * width] = dot(pick, rows_ref[...]).astype(jnp.bfloat16)
        if plan.rest:
            total = None
            for c in range(plan.cuts):
                pick = (slot_of == row % plan.rest + plan.full * SUB) & (row // plan.rest == c)
                part = dot(pick.astype(jnp.bfloat16), rows_ref[:, c * plan.cut : (c + 1) * plan.cut])
                total = part if total is None else total + part
            sbuf[which, :, plan.full * width :] = total.astype(jnp.bfloat16)

    def chunk(dest):
        return pl.ds(pl.multiple_of(dest * SUB, SUB), SUB)

    def landed(dest):
        return pl.ds(pl.multiple_of((member * plan.dests + dest) * SUB, SUB), SUB)

    def sending(which, dest):
        return remote(
            sbuf.at[which, chunk(dest)],
            recv_ref.at[which, landed(mine)],
            send_sem.at[which, dest],
            recv_sem.at[which, mine],
            partner(plan, dest, member),
        )

    def arriving(which, source):
        return remote(
            sbuf.at[which, chunk(source)],
            recv_ref.at[which, landed(source)],
            send_sem.at[which, source],
            recv_sem.at[which, source],
            partner(plan, source, member),
        )

    def send_all(which):
        def step(j, carry):
            sending(which, (mine + j) % plan.dests).start()
            return carry

        lax.fori_loop(1, plan.dests, step, 0)
        recv_ref[which, landed(mine), :] = sbuf[which, chunk(mine), :]

    span = plan.dests // plan.pieces

    def passing(which, piece, other, owner):
        at = pl.ds(pl.multiple_of((owner * plan.dests + piece * span) * SUB, SUB), span * SUB)
        to = (seq // plan.group * plan.group + (member + other) % plan.group, exp)
        return remote(
            recv_ref.at[which, at],
            recv_ref.at[which, at],
            fsend.at[which, piece, other],
            frecv.at[which, piece, owner],
            to,
        )

    def pass_on(which):
        for piece in range(plan.pieces):
            def step(j, carry):
                source = piece * span + j

                @pl.when(source != mine)
                def _():
                    arriving(which, source).wait_recv()

                return carry

            lax.fori_loop(0, span, step, 0)
            for other in range(1, plan.group):
                passing(which, piece, other, member).start()

    def finish(which):
        for piece in range(plan.pieces):
            for other in range(1, plan.group):
                owner = (member + plan.group - other) % plan.group
                passing(which, piece, other, owner).wait_recv()
                passing(which, piece, other, member).wait_send()

        def step(j, carry):
            sending(which, (mine + j) % plan.dests).wait_send()
            return carry

        lax.fori_loop(1, plan.dests, step, 0)

    pack(1, grad_ref)
    send_all(1)

    kx_ref[1] = k_ref[...]
    vx_ref[1] = v_ref[...]
    blank = jnp.zeros((local_len, width), jnp.bfloat16)

    @pl.when(seq == 0)
    def _():
        kx_ref[0] = blank
        vx_ref[0] = blank

    @pl.when(seq == last)
    def _():
        kx_ref[2] = blank
        vx_ref[2] = blank

    mask = window_mask(plan, offs_ref, seq)

    @pl.when(seq > 0)
    def _():
        for c in halo(True):
            c.wait_recv()

    @pl.when(seq < last)
    def _():
        for c in halo(False):
            c.wait_recv()

    per = 4

    def heads(i, carry):
        for u in range(per):
            h = i * per + u
            at = pl.ds(pl.multiple_of(h * HEAD_DIM, HEAD_DIM), HEAD_DIM)
            kh = kx_ref[:, :, at].reshape(3 * local_len, HEAD_DIM)
            vh = vx_ref[:, :, at].reshape(3 * local_len, HEAD_DIM)
            scores = dot(kh, q_ref[:, at], ((1,), (1,))) * HEAD_DIM ** (-0.5)
            scores = jnp.where(mask, scores, -jnp.inf)
            raised = jnp.exp(scores - jnp.max(scores, axis=0, keepdims=True))
            weights = raised / jnp.sum(raised, axis=0, keepdims=True)
            prob_ref[h] = weights
            out_ref[:, at] = dot(weights.astype(jnp.bfloat16), vh, ((0,), (0,)))
        return carry

    lax.fori_loop(0, plan.heads // per, heads, 0)

    attn_out = out_ref[...]
    inv_rms = lax.rsqrt(jnp.mean(attn_out * attn_out, axis=-1, keepdims=True) + epsilon)
    unit = attn_out * inv_rms
    unit_ref[...] = unit
    inv_ref[...] = jnp.broadcast_to(inv_rms, (local_len, 128))
    normed_ref[...] = (unit * gain_ref[...]).astype(jnp.bfloat16)
    pack(0, normed_ref)
    send_all(0)
    pass_on(1)
    pass_on(0)

    @pl.when(seq < last)
    def _():
        for c in halo(True):
            c.wait_send()

    @pl.when(seq > 0)
    def _():
        for c in halo(False):
            c.wait_send()

    finish(1)
    finish(0)


def backward_kernel(
    plan, ids_ref, gates_ref, part_ref, q_ref, grad_ref, gain_ref, prob_ref, unit_ref, inv_ref, vx_ref,
    key_ref, value_ref,
    rbuf, ssum, back, ag_ref, mid_ref, side_ref, side_in,
    send_sem, recv_sem, fsend, frecv, side_send, side_recv,
):
    seq, exp = place()
    local_len, width, rows = plan.local_len, plan.width, plan.rows
    member = seq % plan.group
    mine = seq // plan.group * plan.col_count + exp
    last = plan.seq_count - 1
    greet(plan)
    span = plan.dests // plan.pieces * SUB

    def summing(piece, other):
        to_member = (member + other) % plan.group
        return remote(
            part_ref.at[pl.ds(pl.multiple_of(to_member * rows + piece * span, SUB), span)],
            rbuf.at[other, pl.ds(piece * span, span)],
            fsend.at[piece, other],
            frecv.at[piece, other],
            (seq // plan.group * plan.group + to_member, exp),
        )

    for piece in range(plan.pieces):
        for other in range(1, plan.group):
            summing(piece, other).start()

    def chunk(dest):
        return pl.ds(pl.multiple_of(dest * SUB, SUB), SUB)

    def sending(dest):
        return remote(
            ssum.at[chunk(dest)], back.at[chunk(mine)], send_sem.at[dest], recv_sem.at[mine],
            partner(plan, dest, member),
        )

    def arriving(source):
        return remote(
            ssum.at[chunk(source)], back.at[chunk(source)], send_sem.at[source], recv_sem.at[source],
            partner(plan, source, member),
        )

    for piece in range(plan.pieces):
        for other in range(1, plan.group):
            summing(piece, other).wait_recv()
        at = pl.ds(piece * span, span)
        total = part_ref[pl.ds(pl.multiple_of(member * rows + piece * span, SUB), span), :].astype(jnp.float32)
        for other in range(1, plan.group):
            total = total + rbuf[other, at, :].astype(jnp.float32)
        ssum[at, :] = total.astype(jnp.bfloat16)

        def step(j, carry):
            dest = piece * (span // SUB) + j

            @pl.when(dest != mine)
            def _():
                sending(dest).start()

            return carry

        lax.fori_loop(0, span // SUB, step, 0)
    back[chunk(mine), :] = ssum[chunk(mine), :]

    blank = jnp.zeros((2, local_len, width), jnp.bfloat16)

    @pl.when(seq == 0)
    def _():
        side_in[0] = blank

    @pl.when(seq == last)
    def _():
        side_in[1] = blank

    expert = expert_of(plan, iota((local_len, plan.dests), 1))
    named = [ids_ref[:, j : j + 1] == expert for j in range(2)]
    routed = (named[0] | named[1]).astype(jnp.bfloat16)
    before = (iota((local_len, local_len), 1) < iota((local_len, local_len), 0)).astype(jnp.bfloat16)
    rank = dot(before, routed)
    spread = (iota((plan.dests, rows), 1) // SUB == iota((plan.dests, rows), 0)).astype(jnp.bfloat16)
    row = iota((local_len, rows), 1) % SUB
    slots = [
        dot(jnp.where(named[j], rank, -1.0).astype(jnp.bfloat16), spread).astype(jnp.int32) for j in range(2)
    ]

    def wait_back(j, carry):
        arriving((mine + j) % plan.dests).wait_recv()
        return carry

    lax.fori_loop(1, plan.dests, wait_back, 0)

    pieces = []
    blocks = plan.cuts if plan.rest else 1
    step_width = width // blocks
    for c in range(blocks):
        total = None
        for j in range(2):
            got = None
            for f in range(plan.full):
                pick = (slots[j] == row + f * SUB).astype(jnp.bfloat16)
                part = dot(pick, back[:, f * width + c * step_width : f * width + (c + 1) * step_width])
                got = part if got is None else got + part
            if plan.rest:
                pick = (slots[j] == row % plan.rest + plan.full * SUB) & (row // plan.rest == c)
                part = dot(pick.astype(jnp.bfloat16), back[:, plan.full * width :])
                got = part if got is None else got + part
            got = gates_ref[:, j : j + 1] * got
            total = got if total is None else total + got
        pieces.append(total)
    normed_grad = jnp.concatenate(pieces, axis=1)
    scaled = normed_grad * gain_ref[...]
    unit = unit_ref[...]
    inner = jnp.mean(scaled * unit, axis=-1, keepdims=True)
    attn_grad = grad_ref[...].astype(jnp.float32) + inv_ref[:, 0:1] * (scaled - unit * inner)
    ag_ref[...] = attn_grad.astype(jnp.bfloat16)

    parts = 4
    per = plan.heads // parts

    def side_copy(p, right):
        cols = pl.ds(p * per * HEAD_DIM, per * HEAD_DIM)
        d = 1 if right else 0
        to = (seq + 1, exp) if right else (seq - 1, exp)
        return remote(
            side_ref.at[d, :, :, cols], side_in.at[1 - d, :, :, cols],
            side_send.at[d, p], side_recv.at[1 - d, p], to,
        )

    for p in range(parts):
        for u in range(per):
            h = p * per + u
            at = slice(h * HEAD_DIM, (h + 1) * HEAD_DIM)
            vh = vx_ref[:, :, at].reshape(3 * local_len, HEAD_DIM)
            weights = prob_ref[h]
            grad_h = ag_ref[:, at]
            prob_grad = dot(vh, grad_h, ((1,), (1,)))
            inner_sum = jnp.sum(weights * prob_grad, axis=0, keepdims=True)
            score_grad = (weights * (prob_grad - inner_sum)).astype(jnp.bfloat16)
            key_part = dot(score_grad, q_ref[:, at]) * HEAD_DIM ** (-0.5)
            value_part = dot(weights.astype(jnp.bfloat16), grad_h)
            for i, part in enumerate((key_part, value_part)):
                side_ref[0, i, :, at] = part[:local_len].astype(jnp.bfloat16)
                mid_ref[i, :, at] = part[local_len : 2 * local_len]
                side_ref[1, i, :, at] = part[2 * local_len :].astype(jnp.bfloat16)

        @pl.when(seq > 0)
        def _():
            side_copy(p, False).start()

        @pl.when(seq < last)
        def _():
            side_copy(p, True).start()

    for p in range(parts):
        @pl.when(seq > 0)
        def _():
            side_copy(p, True).wait_recv()

        @pl.when(seq < last)
        def _():
            side_copy(p, False).wait_recv()

        at = slice(p * per * HEAD_DIM, (p + 1) * per * HEAD_DIM)
        for i, ref in enumerate((key_ref, value_ref)):
            total = mid_ref[i, :, at] + side_in[0, i, :, at].astype(jnp.float32)
            ref[:, at] = (total + side_in[1, i, :, at].astype(jnp.float32)).astype(jnp.bfloat16)

    for p in range(parts):
        @pl.when(seq > 0)
        def _():
            side_copy(p, False).wait_send()

        @pl.when(seq < last)
        def _():
            side_copy(p, True).wait_send()

    for piece in range(plan.pieces):
        for other in range(1, plan.group):
            summing(piece, other).wait_send()

    def wait_sent(j, carry):
        sending((mine + j) % plan.dests).wait_send()
        return carry

    lax.fori_loop(1, plan.dests, wait_sent, 0)


def expert_part(rows_in, rows_grad, gate_w, up_w, down_w):
    part_width = gate_w.shape[1]
    both_w = jnp.concatenate([gate_w, up_w], axis=1)
    projected = jnp.dot(rows_in, both_w, preferred_element_type=jnp.float32)
    gate_proj = projected[:, :part_width]
    up_proj = projected[:, part_width:]
    hidden_grad = jnp.einsum("rd,fd->rf", rows_grad, down_w, preferred_element_type=jnp.float32)
    sig = jax.nn.sigmoid(gate_proj)
    grad_up = (hidden_grad * gate_proj * sig).astype(jnp.bfloat16)
    grad_gate = (hidden_grad * up_proj * sig * (1.0 + gate_proj * (1.0 - sig))).astype(jnp.bfloat16)
    both_grad = jnp.concatenate([grad_gate, grad_up], axis=1)
    total = jnp.einsum("rf,df->rd", both_grad, both_w, preferred_element_type=jnp.float32)
    return total.astype(jnp.bfloat16)


def unpacked(plan, packed):
    lead = packed.shape[0] // SUB
    blocks = [packed[:, f * plan.width : (f + 1) * plan.width] for f in range(plan.full)]
    if plan.rest:
        rest = packed[:, plan.full * plan.width :].reshape(lead, plan.cuts, plan.rest, plan.cut)
        blocks.append(rest.transpose(0, 2, 1, 3).reshape(lead * plan.rest, plan.width))
    return jnp.concatenate(blocks, axis=0)


def repacked(plan, rows, lead):
    blocks = [rows[f * lead * SUB : (f + 1) * lead * SUB] for f in range(plan.full)]
    if plan.rest:
        rest = rows[plan.full * lead * SUB :].reshape(lead, plan.rest, plan.cuts, plan.cut)
        blocks.append(rest.transpose(0, 2, 1, 3).reshape(lead * SUB, plan.cut))
    return jnp.concatenate(blocks, axis=1)


def on_device(
    queries,
    keys,
    values,
    out_grad,
    norm_gain,
    gate_values,
    expert_ids,
    tile_offsets,
    gate_weight,
    up_weight,
    down_weight,
):
    local_len, width = queries.shape[1:]
    plan = Plan(local_len, width, lax.axis_size("seq"), lax.axis_size("exp"))
    gain = norm_gain.reshape(1, width)
    group, rows, packed = plan.group, plan.rows, plan.packed
    vmem = pl.BlockSpec(memory_space=pltpu.VMEM)
    smem = pl.BlockSpec(memory_space=pltpu.SMEM)
    bf16, f32 = jnp.bfloat16, jnp.float32
    dma = pltpu.SemaphoreType.DMA
    recv, prob, unit, inv, vx = pl.pallas_call(
        functools.partial(forward_kernel, plan),
        out_shape=(
            jax.ShapeDtypeStruct((2, group * rows, packed), bf16),
            jax.ShapeDtypeStruct((plan.heads, 3 * local_len, local_len), f32),
            jax.ShapeDtypeStruct((local_len, width), f32),
            jax.ShapeDtypeStruct((local_len, 128), f32),
            jax.ShapeDtypeStruct((3, local_len, width), bf16),
        ),
        in_specs=[smem] + [vmem] * 6,
        out_specs=(vmem,) * 5,
        scratch_shapes=[
            pltpu.VMEM((3, local_len, width), bf16),
            pltpu.VMEM((local_len, width), bf16),
            pltpu.VMEM((2, rows, packed), bf16),
            pltpu.VMEM((local_len, width), f32),
            dma((2, 2)),
            dma((2, 2)),
            dma((2, plan.dests)),
            dma((2, plan.dests)),
            dma((2, plan.pieces, group)),
            dma((2, plan.pieces, group)),
        ],
        compiler_params=pltpu.CompilerParams(
            collective_id=0, has_side_effects=True, vmem_limit_bytes=56 * 2**20
        ),
        name="attend_and_dispatch",
    )(tile_offsets[0], expert_ids[0].T, queries[0], keys[0], values[0], out_grad[0], gain)
    partial_value = expert_part(
        unpacked(plan, recv[0]), unpacked(plan, recv[1]), gate_weight[0, 0], up_weight[0, 0], down_weight[0, 0]
    )
    partial_value = repacked(plan, partial_value, group * plan.dests)
    key_out, value_out = pl.pallas_call(
        functools.partial(backward_kernel, plan),
        out_shape=(jax.ShapeDtypeStruct((local_len, width), bf16),) * 2,
        in_specs=[vmem] * 10,
        out_specs=(vmem,) * 2,
        scratch_shapes=[
            pltpu.VMEM((group, rows, packed), bf16),
            pltpu.VMEM((rows, packed), bf16),
            pltpu.VMEM((rows, packed), bf16),
            pltpu.VMEM((local_len, width), bf16),
            pltpu.VMEM((2, local_len, width), f32),
            pltpu.VMEM((2, 2, local_len, width), bf16),
            pltpu.VMEM((2, 2, local_len, width), bf16),
            dma((plan.dests,)),
            dma((plan.dests,)),
            dma((plan.pieces, group)),
            dma((plan.pieces, group)),
            dma((2, 4)),
            dma((2, 4)),
        ],
        compiler_params=pltpu.CompilerParams(
            collective_id=1, has_side_effects=True, vmem_limit_bytes=56 * 2**20
        ),
        name="combine_and_attend_back",
    )(expert_ids[0], gate_values[0], partial_value, queries[0], out_grad[0], gain, prob, unit, inv, vx)
    return (key_out[None], value_out[None])


def solution(mesh):
    return jax.shard_map(
        on_device,
        mesh=mesh,
        in_specs=(
            P("exp", "seq", None),
            P("exp", "seq", None),
            P("exp", "seq", None),
            P("exp", "seq", None),
            P(),
            P("exp", "seq", None),
            P("exp", "seq", None),
            P("exp", "seq", None),
            P("exp", "seq", None, None),
            P("exp", "seq", None, None),
            P("exp", "seq", None, None),
        ),
        out_specs=(P("exp", "seq", None), P("exp", "seq", None)),
        check_vma=False,
    )
```

time: 503 us -> 183 us (0.36)
  the two profiles are of different devices: /device:TPU:1 before, /device:TPU:29 now
where the time goes in v1:
time: 183 us
  Pallas kernels  132 us (72%)
  local copies, waits for them, and re-layouts  26.3 us (14%)
  matrix products  21.9 us (12%)
    pallas_call x1, Pallas kernels, on_device(): pl.pallas_call(functools.partial(forward_kernel, plan), out_shape=(jax.Sh...  71.7 us
    pallas_call x1, Pallas kernels, on_device(): pl.pallas_call(functools.partial(backward_kernel, plan), out_shape=(jax.S...  60.2 us
    dot_general x1, matrix products, expert_part(): projected = jnp.dot(rows_in, both_w, preferred_element_type=jnp.float32)  10.1 us
    unnamed x22, local copies, waits for them, and re-layouts  9.62 us
    dot_general x1, matrix products, expert_part(): jnp.einsum('rd,fd->rf', rows_grad, down_w, preferred_element_type=jnp.flo...  6.18 us
    dot_general x1, matrix products, expert_part(): jnp.einsum('rf,df->rd', both_grad, both_w, preferred_element_type=jnp.flo...  5.6 us

profile of v1, /device:TPU:29, one launch (start us, length us, event | category | flops | bytes accessed | tf_op | source)
XLA Modules:
  0.0 182.6 jit_solution(11201103137642167823)
XLA Ops:
  0.6 0.8 copy.13
  2.1 71.7 %attend_and_dispatch.1 = (bf16[2,512,2560]{2,1,0:T(8,128)(2,1)}, f32[16,384,128]{2,1,0:T(8,128)}, f32[128,2048]{1,0:T(8,128)}, f32[128,128]{1,0:T(8,128)}, bf16[3,128,2048]{2,1,0:T(8,128)(2,1)}) custom-call(s32[2,3]{1,0:T(2,128)} %bitcast.54, s32[2,128]{1,0:T(2,128)} %copy.15.ids_ref, bf16[128,2048]{1,0:T(8,128)(2,1)} %bitcast.34, ...), custom_call_target="tpu_custom_call" | custom-call | tf_op jit(solution)/shard_map/attend_and_dispatch/pallas_call | solution.py:552
  73.8 2.9 %slice_bitcast_fusion = (bf16[512,2560]{1,0:T(8,128)(2,1)S(1)}, bf16[512,2560]{1,0:T(8,128)(2,1)S(1)}) fusion(bf16[2,512,2560]{2,1,0:T(8,128)(2,1)} %get-tuple-element.9), kind=kLoop, calls=%fused_computation.22 | loop fusion | bytes 10485760 | tf_op jit(solution)/shard_map/squeeze | solution.py:581
  76.7 1.5 copy-done
  78.2 0.8 slice.43
  79.0 1.2 reshape.28
  80.6 1.9 %slice.42 = bf16[512,2048]{1,0:T(8,128)(2,1)S(1)} slice(bf16[512,2560]{1,0:T(8,128)(2,1)} %copy-done), slice={[0:512], [0:2048]} | slice | bytes 4194304 | tf_op jit(solution)/shard_map/slice | solution.py:516
  82.5 0.8 copy-done.5
  83.3 10.1 %fusion.1 = f32[640,2048]{1,0:T(8,128)} fusion(bf16[2048,1024]{1,0:T(8,128)(2,1)S(1)} %bitcast.55, bf16[2048,1024]{1,0:T(8,128)(2,1)} %bitcast.57, bf16[128,2048]{1,0:T(8,128)(2,1)S(1)} %bitcast.50, bf16[512,2048]{1,0:T(8,128)(2,1)S(1)} %slice.42), kind=kOutput, calls=%fused_computation.2 | convolution fusion | flops 5390729216 | bytes 16252928 | tf_op jit(solution)/shard_map/dot_general | solution.py:502
  93.4 0.8 slice.41
  94.2 1.2 reshape.26
  96.1 1.8 copy-done.4
  97.9 6.2 %fusion.7 = (bf16[640,1024]{1,0:T(8,128)(2,1)S(1)}, bf16[640,1024]{1,0:T(8,128)(2,1)S(1)}) fusion(f32[640,2048]{1,0:T(8,128)} %fusion.1, bf16[1,1,1024,2048]{3,2,1,0:T(8,128)(2,1)S(1)} %copy-done.4, bf16[128,2048]{1,0:T(8,128)(2,1)S(1)} %bitcast.49, bf16[512,2048]{1,0:T(8,128)(2,1)S(1)} %slice.40), kind=kOutput, calls=%fused_computation.9 | convolution fusion | flops 2698117120 | bytes 14680064 | tf_op jit(solution)/shard_map/rd,fd->rf/dot_general | solution.py:505
  104.1 5.6 %fusion.4 = bf16[640,2048]{1,0:T(8,128)(2,1)S(1)} fusion(bf16[2048,1024]{1,0:T(8,128)(2,1)S(1)} %bitcast.56, bf16[2048,1024]{1,0:T(8,128)(2,1)S(1)} %bitcast.58, bf16[640,1024]{1,0:T(8,128)(2,1)S(1)} %get-tuple-element.17, bf16[640,1024]{1,0:T(8,128)(2,1)S(1)} %get-tuple-element.16), kind=kOutput, calls=%fused_computation.5 | convolution fusion | flops 5392039936 | bytes 13631488 | tf_op jit(solution)/shard_map/rf,df->rd/dot_general | solution.py:510
  109.7 0.9 slice.47
  110.6 1.6 reshape.30
  112.2 1.1 copy.22
  113.2 1.2 reshape.31
  114.4 1.8 %slice.46 = bf16[512,2048]{1,0:T(8,128)(2,1)S(1)} slice(bf16[640,2048]{1,0:T(8,128)(2,1)} %copy-done.1), slice={[0:512], [0:2048]} | slice | bytes 4194304 | tf_op jit(solution)/shard_map/slice | solution.py:524
  116.3 1.7 pad_maximum_fusion.5.part_ref
  118.0 0.7 copy.14
  118.7 60.2 %combine_and_attend_back.1 = (bf16[128,2048]{1,0:T(8,128)(2,1)}, bf16[128,2048]{1,0:T(8,128)(2,1)}) custom-call(s32[128,2]{1,0:T(8,128)} %bitcast.44, f32[128,2]{1,0:T(8,128)} %bitcast.51, bf16[512,2560]{1,0:T(8,128)(2,1)} %pad_maximum_fusion.5.part_ref, bf16[128,2048]{1,0:T(8,128)(2,1)} %bitcast.35, bf16[128,2048]{1,0:T(8,128)(2,1)} %bitcast.37, ...), custom_call_target="tpu_custom_call" | custom-call | tf_op jit(solution)/shard_map/combine_and_attend_back/pallas_call | solution.py:584
  178.9 1.9 %copy.25 = bf16[1,128,2048]{2,1,0:T(8,128)(2,1)} copy(bf16[1,128,2048]{2,1,0:T(8,128)(2,1)} %bitcast.48) | data formatting | bytes 1048576
  180.8 1.9 %copy.26 = bf16[1,128,2048]{2,1,0:T(8,128)(2,1)} copy(bf16[1,128,2048]{2,1,0:T(8,128)(2,1)} %bitcast.47) | data formatting | bytes 1048576
  (19 shorter events, 1.7 us)
Async XLA Ops:
  1.4 75.3 %copy-start.2 = (s32[1,128,2]{2,1,0:T(8,128)}, s32[1,128,2]{2,1,0:T(8,128)S(1)}, u32[]{:S(2)}) copy-start(s32[1,128,2]{2,1,0:T(8,128)S(1)} %copy.13) | copy-start | bytes 3076
  76.7 1.5 copy-start
  80.5 2.8 %copy-start.5 = (bf16[1,1,2048,1024]{3,2,1,0:T(8,128)(2,1)S(1)}, bf16[1,1,2048,1024]{3,2,1,0:T(8,128)(2,1)}, u32[]{:S(2)}) copy-start(bf16[1,1,2048,1024]{3,2,1,0:T(8,128)(2,1)} %param.20) | copy-start | bytes 12582916
  95.7 2.2 %copy-start.4 = (bf16[1,1,1024,2048]{3,2,1,0:T(8,128)(2,1)S(1)}, bf16[1,1,1024,2048]{3,2,1,0:T(8,128)(2,1)}, u32[]{:S(2)}) copy-start(bf16[1,1,1024,2048]{3,2,1,0:T(8,128)(2,1)} %param.21) | copy-start | bytes 12582916
  97.9 6.2 %copy-start.6 = (bf16[1,1,2048,1024]{3,2,1,0:T(8,128)(2,1)S(1)}, bf16[1,1,2048,1024]{3,2,1,0:T(8,128)(2,1)}, u32[]{:S(2)}) copy-start(bf16[1,1,2048,1024]{3,2,1,0:T(8,128)(2,1)} %param.20) | copy-start | bytes 12582916
  97.9 6.2 %copy-start.7 = (bf16[1,1,2048,1024]{3,2,1,0:T(8,128)(2,1)S(1)}, bf16[1,1,2048,1024]{3,2,1,0:T(8,128)(2,1)}, u32[]{:S(2)}) copy-start(bf16[1,1,2048,1024]{3,2,1,0:T(8,128)(2,1)} %param.19) | copy-start | bytes 12582916
  109.7 3.6 %copy-start.1 = (bf16[640,2048]{1,0:T(8,128)(2,1)}, bf16[640,2048]{1,0:T(8,128)(2,1)S(1)}, u32[]{:S(2)}) copy-start(bf16[640,2048]{1,0:T(8,128)(2,1)S(1)} %fusion.4) | copy-start | bytes 7864324
  116.2 1.7 copy-start.3

commit v2 on v1

--- a/solution.py
+++ b/solution.py
@@ -42,6 +42,9 @@
         self.dests = 2 * col_count
         self.rows = self.dests * SUB
         self.pieces = 4
+        self.lead = min(32, self.group * self.dests)
+        self.blocks = self.group * self.dests // self.lead
+        self.block_rows = self.lead * (self.full * SUB + self.rest)
 
 
 def expert_of(plan, dest):
@@ -112,9 +115,10 @@
 
 
 def forward_kernel(
-    plan, offs_ref, ids_ref, q_ref, k_ref, v_ref, grad_ref, gain_ref,
-    recv_ref, prob_ref, unit_ref, inv_ref, vx_ref,
-    kx_ref, normed_ref, sbuf, out_ref,
+    plan, offs_ref, ids_ref, q_ref, k_ref, v_ref, grad_ref, gain_ref, gate_hbm, up_hbm, down_hbm,
+    part_ref, prob_ref, unit_ref, inv_ref, vx_ref,
+    recv_ref, kx_ref, normed_ref, sbuf, out_ref,
+    gate_ref, up_ref, down_ref, rows_ref, hidden_ref, both_ref, weight_sem,
     halo_send, halo_recv, send_sem, recv_sem, fsend, frecv,
 ):
     seq, exp = place()
@@ -122,6 +126,12 @@
     member = seq % plan.group
     mine = seq // plan.group * plan.col_count + exp
     last = plan.seq_count - 1
+    weights = [
+        pltpu.make_async_copy(src, dst, weight_sem.at[i])
+        for i, (src, dst) in enumerate(((down_hbm, down_ref), (gate_hbm, gate_ref), (up_hbm, up_ref)))
+    ]
+    for c in weights:
+        c.start()
     greet(plan)
 
     def halo(right):
@@ -224,11 +234,15 @@
             for other in range(1, plan.group):
                 passing(which, piece, other, member).start()
 
-    def finish(which):
+    def forwarded(which):
         for piece in range(plan.pieces):
             for other in range(1, plan.group):
                 owner = (member + plan.group - other) % plan.group
                 passing(which, piece, other, owner).wait_recv()
+
+    def finish(which):
+        for piece in range(plan.pieces):
+            for other in range(1, plan.group):
                 passing(which, piece, other, member).wait_send()
 
         def step(j, carry):
@@ -292,8 +306,90 @@
     normed_ref[...] = (unit * gain_ref[...]).astype(jnp.bfloat16)
     pack(0, normed_ref)
     send_all(0)
+    lead, full_rows = plan.lead, plan.lead * plan.full * SUB
+    rest_rows, block = plan.lead * plan.rest, plan.block_rows
+    hidden_width = gate_ref.shape[1]
+
+    def rest_pick(cut, shape, out_dim):
+        out, into = iota(shape, out_dim), iota(shape, 1 - out_dim)
+        return (
+            (into // SUB == out // plan.rest) & (into % SUB == cut * plan.rest + out % plan.rest)
+        ).astype(jnp.bfloat16)
+
+    def unpack(which, b):
+        at = pl.ds(pl.multiple_of(b * lead * SUB, SUB), lead * SUB)
+        for f in range(plan.full):
+            rows_ref[f * lead * SUB : (f + 1) * lead * SUB, :] = recv_ref[
+                which, at, f * width : (f + 1) * width
+            ]
+        for c in range(plan.cuts):
+            pick = rest_pick(c, (rest_rows, lead * SUB), 0)
+            rows_ref[full_rows:, c * plan.cut : (c + 1) * plan.cut] = dot(
+                pick, recv_ref[which, at, plan.full * width :]
+            ).astype(jnp.bfloat16)
+
+    def repack(b):
+        at = pl.ds(pl.multiple_of(b * lead * SUB, SUB), lead * SUB)
+        for f in range(plan.full):
+            part_ref[at, f * width : (f + 1) * width] = rows_ref[f * lead * SUB : (f + 1) * lead * SUB, :]
+        if plan.rest:
+            total = None
+            for c in range(plan.cuts):
+                pick = rest_pick(c, (lead * SUB, rest_rows), 1)
+                part = dot(pick, rows_ref[full_rows:, c * plan.cut : (c + 1) * plan.cut])
+                total = part if total is None else total + part
+            part_ref[at, plan.full * width :] = total.astype(jnp.bfloat16)
+
+    tile = 256
+
+    def cols(i):
+        return pl.ds(pl.multiple_of(i * tile, tile), tile)
+
+    def hidden_block(b, carry):
+        unpack(1, b)
+        at = pl.ds(pl.multiple_of(b * block, SUB), block)
+
+        def step(i, inner):
+            hidden_ref[at, cols(i)] = dot(rows_ref[...], down_ref[cols(i), :], ((1,), (1,)))
+            return inner
+
+        return lax.fori_loop(0, hidden_width // tile, step, carry)
+
+    def expert_block(b, carry):
+        unpack(0, b)
+        at = pl.ds(pl.multiple_of(b * block, SUB), block)
+
+        def project(i, inner):
+            gate_proj = dot(rows_ref[...], gate_ref[:, cols(i)])
+            up_proj = dot(rows_ref[...], up_ref[:, cols(i)])
+            hidden_grad = hidden_ref[at, cols(i)]
+            sig = jax.nn.sigmoid(gate_proj)
+            scaled = hidden_grad * sig
+            both_ref[0, :, cols(i)] = (scaled * up_proj * (1.0 + gate_proj * (1.0 - sig))).astype(jnp.bfloat16)
+            both_ref[1, :, cols(i)] = (scaled * gate_proj).astype(jnp.bfloat16)
+            return inner
+
+        lax.fori_loop(0, hidden_width // tile, project, 0)
+
+        def collect(i, inner):
+            total = dot(both_ref[0], gate_ref[cols(i), :], ((1,), (1,)))
+            total = total + dot(both_ref[1], up_ref[cols(i), :], ((1,), (1,)))
+            rows_ref[:, cols(i)] = total.astype(jnp.bfloat16)
+            return inner
+
+        lax.fori_loop(0, width // tile, collect, 0)
+        repack(b)
+        return carry
+
     pass_on(1)
+    forwarded(1)
+    weights[0].wait()
+    lax.fori_loop(0, plan.blocks, hidden_block, 0)
     pass_on(0)
+    weights[1].wait()
+    weights[2].wait()
+    forwarded(0)
+    lax.fori_loop(0, plan.blocks, expert_block, 0)
 
     @pl.when(seq < last)
     def _():
@@ -496,38 +592,6 @@
     lax.fori_loop(1, plan.dests, wait_sent, 0)
 
 
-def expert_part(rows_in, rows_grad, gate_w, up_w, down_w):
-    part_width = gate_w.shape[1]
-    both_w = jnp.concatenate([gate_w, up_w], axis=1)
-    projected = jnp.dot(rows_in, both_w, preferred_element_type=jnp.float32)
-    gate_proj = projected[:, :part_width]
-    up_proj = projected[:, part_width:]
-    hidden_grad = jnp.einsum("rd,fd->rf", rows_grad, down_w, preferred_element_type=jnp.float32)
-    sig = jax.nn.sigmoid(gate_proj)
-    grad_up = (hidden_grad * gate_proj * sig).astype(jnp.bfloat16)
-    grad_gate = (hidden_grad * up_proj * sig * (1.0 + gate_proj * (1.0 - sig))).astype(jnp.bfloat16)
-    both_grad = jnp.concatenate([grad_gate, grad_up], axis=1)
-    total = jnp.einsum("rf,df->rd", both_grad, both_w, preferred_element_type=jnp.float32)
-    return total.astype(jnp.bfloat16)
-
-
-def unpacked(plan, packed):
-    lead = packed.shape[0] // SUB
-    blocks = [packed[:, f * plan.width : (f + 1) * plan.width] for f in range(plan.full)]
-    if plan.rest:
-        rest = packed[:, plan.full * plan.width :].reshape(lead, plan.cuts, plan.rest, plan.cut)
-        blocks.append(rest.transpose(0, 2, 1, 3).reshape(lead * plan.rest, plan.width))
-    return jnp.concatenate(blocks, axis=0)
-
-
-def repacked(plan, rows, lead):
-    blocks = [rows[f * lead * SUB : (f + 1) * lead * SUB] for f in range(plan.full)]
-    if plan.rest:
-        rest = rows[plan.full * lead * SUB :].reshape(lead, plan.rest, plan.cuts, plan.cut)
-        blocks.append(rest.transpose(0, 2, 1, 3).reshape(lead * SUB, plan.cut))
-    return jnp.concatenate(blocks, axis=1)
-
-
 def on_device(
     queries,
     keys,
@@ -548,23 +612,32 @@
     vmem = pl.BlockSpec(memory_space=pltpu.VMEM)
     smem = pl.BlockSpec(memory_space=pltpu.SMEM)
     bf16, f32 = jnp.bfloat16, jnp.float32
+    hidden = gate_weight.shape[3]
     dma = pltpu.SemaphoreType.DMA
-    recv, prob, unit, inv, vx = pl.pallas_call(
+    partial_value, prob, unit, inv, vx = pl.pallas_call(
         functools.partial(forward_kernel, plan),
         out_shape=(
-            jax.ShapeDtypeStruct((2, group * rows, packed), bf16),
+            jax.ShapeDtypeStruct((group * rows, packed), bf16),
             jax.ShapeDtypeStruct((plan.heads, 3 * local_len, local_len), f32),
             jax.ShapeDtypeStruct((local_len, width), f32),
             jax.ShapeDtypeStruct((local_len, 128), f32),
             jax.ShapeDtypeStruct((3, local_len, width), bf16),
         ),
-        in_specs=[smem] + [vmem] * 6,
+        in_specs=[smem] + [vmem] * 6 + [pl.BlockSpec(memory_space=pl.ANY)] * 3,
         out_specs=(vmem,) * 5,
         scratch_shapes=[
+            pltpu.VMEM((2, group * rows, packed), bf16),
             pltpu.VMEM((3, local_len, width), bf16),
             pltpu.VMEM((local_len, width), bf16),
             pltpu.VMEM((2, rows, packed), bf16),
             pltpu.VMEM((local_len, width), f32),
+            pltpu.VMEM((width, hidden), bf16),
+            pltpu.VMEM((width, hidden), bf16),
+            pltpu.VMEM((hidden, width), bf16),
+            pltpu.VMEM((plan.block_rows, width), bf16),
+            pltpu.VMEM((plan.blocks * plan.block_rows, hidden), f32),
+            pltpu.VMEM((2, plan.block_rows, hidden), bf16),
+            dma((3,)),
             dma((2, 2)),
             dma((2, 2)),
             dma((2, plan.dests)),
@@ -573,14 +646,13 @@
             dma((2, plan.pieces, group)),
         ],
         compiler_params=pltpu.CompilerParams(
-            collective_id=0, has_side_effects=True, vmem_limit_bytes=56 * 2**20
+            collective_id=0, has_side_effects=True, vmem_limit_bytes=60 * 2**20
         ),
         name="attend_and_dispatch",
-    )(tile_offsets[0], expert_ids[0].T, queries[0], keys[0], values[0], out_grad[0], gain)
-    partial_value = expert_part(
-        unpacked(plan, recv[0]), unpacked(plan, recv[1]), gate_weight[0, 0], up_weight[0, 0], down_weight[0, 0]
+    )(
+        tile_offsets[0], expert_ids[0].T, queries[0], keys[0], values[0], out_grad[0], gain,
+        gate_weight[0, 0], up_weight[0, 0], down_weight[0, 0],
     )
-    partial_value = repacked(plan, partial_value, group * plan.dests)
     key_out, value_out = pl.pallas_call(
         functools.partial(backward_kernel, plan),
         out_shape=(jax.ShapeDtypeStruct((local_len, width), bf16),) * 2,
@@ -602,7 +674,7 @@
             dma((2, 4)),
         ],
         compiler_params=pltpu.CompilerParams(
-            collective_id=1, has_side_effects=True, vmem_limit_bytes=56 * 2**20
+            collective_id=1, has_side_effects=True, vmem_limit_bytes=60 * 2**20
         ),
         name="combine_and_attend_back",
     )(expert_ids[0], gate_values[0], partial_value, queries[0], out_grad[0], gain, prob, unit, inv, vx)

time: 183 us -> 151 us (0.83)
  the two profiles are of different devices: /device:TPU:29 before, /device:TPU:1 now
where the time goes in v2:
time: 151 us; the launch traced here: 148 us
  Pallas kernels  141 us (93%)
  local copies, waits for them, and re-layouts  6.56 us (4%)
    pallas_call x1, Pallas kernels, on_device(): pl.pallas_call(functools.partial(forward_kernel, plan), out_shape=(jax.Sh...  84.2 us
    pallas_call x1, Pallas kernels, on_device(): pl.pallas_call(functools.partial(backward_kernel, plan), out_shape=(jax.S...  56.7 us
    unnamed x6, local copies, waits for them, and re-layouts  5.96 us

profile of v2, /device:TPU:1, one launch (start us, length us, event | category | flops | bytes accessed | tf_op | source)
XLA Modules:
  0.0 148.2 jit_solution(11835522681816070037)
XLA Ops:
  0.6 0.8 copy.13
  1.4 0.0 copy-start
  1.4 0.6 copy.15.ids_ref
  2.0 1.4 copy.14
  3.4 84.2 %attend_and_dispatch.1 = (bf16[512,2560]{1,0:T(8,128)(2,1)}, f32[16,384,128]{2,1,0:T(8,128)}, f32[128,2048]{1,0:T(8,128)}, f32[128,128]{1,0:T(8,128)}, bf16[3,128,2048]{2,1,0:T(8,128)(2,1)}) custom-call(s32[2,3]{1,0:T(2,128)} %bitcast.31, s32[2,128]{1,0:T(2,128)} %copy.15.ids_ref, bf16[128,2048]{1,0:T(8,128)(2,1)} %bitcast.18, bf16[128,2048]{1,0:T(8,128)(2,1)} %bitcast.24, ...), custom_call_target="tpu_custom_call" | custom-call | tf_op jit(solution)/shard_map/attend_and_dispatch/pallas_call | solution.py:617
  87.7 0.0 copy-done
  87.7 56.7 %combine_and_attend_back.1 = (bf16[128,2048]{1,0:T(8,128)(2,1)}, bf16[128,2048]{1,0:T(8,128)(2,1)}) custom-call(s32[128,2]{1,0:T(8,128)} %bitcast.23, f32[128,2]{1,0:T(8,128)} %bitcast.28, bf16[512,2560]{1,0:T(8,128)(2,1)} %get-tuple-element.9.part_ref, bf16[128,2048]{1,0:T(8,128)(2,1)} %bitcast.19, bf16[128,2048]{1,0:T(8,128)(2,1)} %bitcast.21, ...), custom_call_target="tpu_custom_call" | custom-call | tf_op jit(solution)/shard_map/combine_and_attend_back/pallas_call | solution.py:656
  144.4 1.9 %copy.18 = bf16[1,128,2048]{2,1,0:T(8,128)(2,1)} copy(bf16[1,128,2048]{2,1,0:T(8,128)(2,1)} %bitcast.27) | data formatting | bytes 1048576
  146.3 1.9 %copy.19 = bf16[1,128,2048]{2,1,0:T(8,128)(2,1)} copy(bf16[1,128,2048]{2,1,0:T(8,128)(2,1)} %bitcast.26) | data formatting | bytes 1048576
Async XLA Ops:
  1.4 86.3 %copy-start = (s32[1,128,2]{2,1,0:T(8,128)}, s32[1,128,2]{2,1,0:T(8,128)S(1)}, u32[]{:S(2)}) copy-start(s32[1,128,2]{2,1,0:T(8,128)S(1)} %copy.13) | copy-start | bytes 3076

commit v3 on v2

--- a/solution.py
+++ b/solution.py
@@ -220,7 +220,9 @@
         )
 
     def pass_on(which):
-        for piece in range(plan.pieces):
+        for k in range(plan.pieces):
+            piece = (mine // span + plan.pieces - k) % plan.pieces
+
             def step(j, carry):
                 source = piece * span + j
 
@@ -423,15 +425,20 @@
         to_member = (member + other) % plan.group
         return remote(
             part_ref.at[pl.ds(pl.multiple_of(to_member * rows + piece * span, SUB), span)],
-            rbuf.at[other, pl.ds(piece * span, span)],
+            rbuf.at[other, pl.ds(pl.multiple_of(piece * span, SUB), span)],
             fsend.at[piece, other],
             frecv.at[piece, other],
             (seq // plan.group * plan.group + to_member, exp),
         )
 
-    for piece in range(plan.pieces):
+    chunks = span // SUB
+
+    def turn(k):
+        return (mine // chunks + k) % plan.pieces
+
+    for k in range(plan.pieces):
         for other in range(1, plan.group):
-            summing(piece, other).start()
+            summing(turn(k), other).start()
 
     def chunk(dest):
         return pl.ds(pl.multiple_of(dest * SUB, SUB), SUB)
@@ -448,17 +455,18 @@
             partner(plan, source, member),
         )
 
-    for piece in range(plan.pieces):
+    for k in range(plan.pieces):
+        piece = turn(k)
         for other in range(1, plan.group):
             summing(piece, other).wait_recv()
-        at = pl.ds(piece * span, span)
+        at = pl.ds(pl.multiple_of(piece * span, SUB), span)
         total = part_ref[pl.ds(pl.multiple_of(member * rows + piece * span, SUB), span), :].astype(jnp.float32)
         for other in range(1, plan.group):
             total = total + rbuf[other, at, :].astype(jnp.float32)
         ssum[at, :] = total.astype(jnp.bfloat16)
 
-        def step(j, carry):
-            dest = piece * (span // SUB) + j
+        def step(j, carry, piece=piece):
+            dest = piece * chunks + (mine + j) % chunks
 
             @pl.when(dest != mine)
             def _():
@@ -466,7 +474,7 @@
 
             return carry
 
-        lax.fori_loop(0, span // SUB, step, 0)
+        lax.fori_loop(0, chunks, step, 0)
     back[chunk(mine), :] = ssum[chunk(mine), :]
 
     blank = jnp.zeros((2, local_len, width), jnp.bfloat16)

time: 151 us -> 151 us (level); the launches traced: 148 us -> 151 us
  Pallas kernels: 141 us -> 143 us
    pallas_call x1, Pallas kernels: 56.7 us -> 60.1 us  [on_device(): pl.pallas_call(functools.partial(backward_kernel, plan), out_shape=(jax.S...]
where the time goes in v3:
time: 151 us
  Pallas kernels  143 us (95%)
  local copies, waits for them, and re-layouts  6.56 us (4%)
    pallas_call x1, Pallas kernels, on_device(): pl.pallas_call(functools.partial(forward_kernel, plan), out_shape=(jax.Sh...  83.3 us
    pallas_call x1, Pallas kernels, on_device(): pl.pallas_call(functools.partial(backward_kernel, plan), out_shape=(jax.S...  60.1 us
    unnamed x6, local copies, waits for them, and re-layouts  5.96 us

profile of v3, /device:TPU:1, one launch (start us, length us, event | category | flops | bytes accessed | tf_op | source)
XLA Modules:
  0.0 150.6 jit_solution(15770064236835473617)
XLA Ops:
  0.6 0.8 copy.13
  1.4 0.0 copy-start
  1.4 0.6 copy.15.ids_ref
  2.0 1.4 copy.14
  3.4 83.3 %attend_and_dispatch.1 = (bf16[512,2560]{1,0:T(8,128)(2,1)}, f32[16,384,128]{2,1,0:T(8,128)}, f32[128,2048]{1,0:T(8,128)}, f32[128,128]{1,0:T(8,128)}, bf16[3,128,2048]{2,1,0:T(8,128)(2,1)}) custom-call(s32[2,3]{1,0:T(2,128)} %bitcast.31, s32[2,128]{1,0:T(2,128)} %copy.15.ids_ref, bf16[128,2048]{1,0:T(8,128)(2,1)} %bitcast.18, bf16[128,2048]{1,0:T(8,128)(2,1)} %bitcast.24, ...), custom_call_target="tpu_custom_call" | custom-call | tf_op jit(solution)/shard_map/attend_and_dispatch/pallas_call | solution.py:625
  86.7 0.0 copy-done
  86.8 60.1 %combine_and_attend_back.1 = (bf16[128,2048]{1,0:T(8,128)(2,1)}, bf16[128,2048]{1,0:T(8,128)(2,1)}) custom-call(s32[128,2]{1,0:T(8,128)} %bitcast.23, f32[128,2]{1,0:T(8,128)} %bitcast.28, bf16[512,2560]{1,0:T(8,128)(2,1)} %get-tuple-element.9.part_ref, bf16[128,2048]{1,0:T(8,128)(2,1)} %bitcast.19, bf16[128,2048]{1,0:T(8,128)(2,1)} %bitcast.21, ...), custom_call_target="tpu_custom_call" | custom-call | tf_op jit(solution)/shard_map/combine_and_attend_back/pallas_call | solution.py:664
  146.8 1.9 %copy.18 = bf16[1,128,2048]{2,1,0:T(8,128)(2,1)} copy(bf16[1,128,2048]{2,1,0:T(8,128)(2,1)} %bitcast.27) | data formatting | bytes 1048576
  148.7 1.9 %copy.19 = bf16[1,128,2048]{2,1,0:T(8,128)(2,1)} copy(bf16[1,128,2048]{2,1,0:T(8,128)(2,1)} %bitcast.26) | data formatting | bytes 1048576
Async XLA Ops:
  1.4 85.3 %copy-start = (s32[1,128,2]{2,1,0:T(8,128)}, s32[1,128,2]{2,1,0:T(8,128)S(1)}, u32[]{:S(2)}) copy-start(s32[1,128,2]{2,1,0:T(8,128)S(1)} %copy.13) | copy-start | bytes 3076
